TPU v7x, 32 devices: a whole 2x2x4 slice. The times are simulated.
32 devices in a mesh: row: 8 (over y, x, core), col: 4 (over z).
Axes of the slice: x: 2, y: 2, z: 4, core: 2. Of those that a mesh axis runs over, the one named last changes fastest.
Arguments:
- tiles: bfloat16 [8, 4, 80, 256, 256], P('row', 'col'), may hold values from -0.125 to 0.125
- tile_coords: int32 [2, 8, 4, 80], P(None, 'row', 'col'), may hold values from 0 to 1023, as said below
- tile_counts: int32 [8, 4], P('row', 'col'), may hold values from 40 to 80, as said below
- vectors: bfloat16 [262144, 16], P(('row', 'col')), may hold values from -6 to 6
Outputs:
- product: float32 [262144, 16], P(('row', 'col'))
Inputs may be any that keep to these rules, and one draw needn't show every extreme that they name: `tile_coords`: for slot s below tile_counts[r, c]: the tile row I lies in r * 128 to (r + 1) * 128 - 1; the tile column J has (J // 32) % 4 equal to c; when I != J, I < J exactly when I + J is even; no (row, column) pair appears in two live slots anywhere. Among the live slots of one device at most 35 have tile rows in any one run of 32 tile rows, and at most 28 have tile columns in any one run of 32 tile columns; a device with all slots live reaches both. Slots at or above the count hold 0. `tile_counts`: some device holds exactly 80 live slots.
All inputs are finite; a program needn't handle non-finite values.
Results may differ from a plain program's by a relative error of at most 0.0075.
Values may be sent and summed in bfloat16 or wider, within the bound.
A program may use at most 320 MiB of HBM per device.

v0:
```python
import functools

import jax
import jax.numpy as jnp
from jax import lax
from jax.experimental import pallas as pl
from jax.experimental.pallas import tpu as pltpu
from jax.sharding import PartitionSpec as P

MESH = pl.DeviceIdType.MESH
VMEM_LIMIT = 48 * 1024 * 1024
GROUP = 8


def fused_kernel(
    coords, count, coords_v, x_ref, t_ref, o_ref,
    mine, xr, xc, upper, lower, tri, made, keys, onehot, f_ref, m_ref,
    from_sib, chip_out, chip_in, r_out, r_in, l_out, l_in,
    tile_sem, own_sem, zs, zr, gs, gr, ss, sr, fs, fr, bs, br, cs, cr, rs, rr, ls, lr,
):
    r, c = lax.axis_index("row"), lax.axis_index("col")
    chip, core = r // 2, r % 2
    sib = 2 * chip + 1 - core
    slots, tile = upper.shape[0], upper.shape[1]
    vecs, width = x_ref.shape
    per_slab = width // tile
    groups = slots // GROUP
    f32, bf16, i32 = jnp.float32, jnp.bfloat16, jnp.int32

    for p in range(per_slab):
        mine[p] = x_ref[:, p * tile : (p + 1) * tile]

    def slab(i):
        return pl.ds(i * per_slab, per_slab)

    def chip_at(d):
        return (chip + d) % 4

    def tile_copy(g):
        at = pl.ds(g * GROUP, GROUP)
        return pltpu.make_async_copy(t_ref.at[0, 0, at], lower.at[at], tile_sem.at[g])

    barrier = pltpu.get_barrier_semaphore()
    for d in range(1, 4):
        pl.semaphore_signal(barrier, inc=1, device_id=(r, (c + d) % 4), device_id_type=MESH)
        pl.semaphore_signal(
            barrier, inc=1, device_id=(2 * chip_at(d) + core, c), device_id_type=MESH
        )
    pl.semaphore_signal(barrier, inc=1, device_id=(sib, c), device_id_type=MESH)
    pl.semaphore_wait(barrier, 7)

    def remote(src, dst, send, recv, row, col):
        return pltpu.make_async_remote_copy(
            src, dst, send, recv, device_id=(row, col), device_id_type=MESH
        )

    def z_copy(d, slot):
        return remote(mine, xr.at[slab(slot)], zs.at[d], zr.at[d], r, (c + d) % 4)

    def chip_copy(d, slot):
        return remote(mine, xc.at[slab(slot)], gs.at[d], gr.at[d], 2 * chip_at(d) + core, c)

    def sib_copy(slot):
        return remote(mine, xc.at[slab(slot)], ss, sr, sib, c)

    def fwd_copy(d, slot):
        return remote(xc.at[slab(slot)], xc.at[slab(slot)], fs.at[d], fr.at[d], sib, c)

    def right(d, src):
        return remote(src, r_in.at[d], rs.at[d], rr.at[d], r, c + 1)

    def left(d, src):
        return remote(src, l_in.at[d], ls.at[d], lr.at[d], r, c - 1)

    def to_sib(d):
        return remote(
            m_ref.at[2 * chip_at(d) + 1 - core], from_sib.at[d], bs.at[d], br.at[d], sib, c
        )

    def to_chip(d):
        return remote(
            chip_out.at[d], chip_in.at[d], cs.at[d], cr.at[d], 2 * chip_at(d) + core, c
        )

    for d in (2, 1, 3):
        chip_copy(d, r).start()
        z_copy(d, c).start()
    sib_copy(r).start()
    own_r = pltpu.make_async_copy(mine, xr.at[slab(c)], own_sem.at[0])
    own_c = pltpu.make_async_copy(mine, xc.at[slab(r)], own_sem.at[1])
    own_r.start()
    own_c.start()

    def start_tiles(g, _):
        tile_copy(g).start()
        return 0

    lax.fori_loop(0, groups, start_tiles, 0)

    tile_row, tile_col = coords_v[0, 0], coords_v[1, 0]
    live = lax.broadcasted_iota(i32, (1, slots), 1) < count[0, 0]
    span = 4 * per_slab
    places = (tile_row % span, tile_col // span * per_slab + tile_col % per_slab)
    wide = slots * vecs
    spread = lax.broadcasted_iota(i32, (slots, wide), 1) // vecs
    spread = (spread == lax.broadcasted_iota(i32, (slots, wide), 0)).astype(f32).astype(bf16)
    across = lax.broadcasted_iota(i32, (vecs, wide), 1) % vecs
    same = across == lax.broadcasted_iota(i32, (vecs, wide), 0)
    for k in range(2):
        place = jnp.where(live, places[k], -1).astype(f32)
        place = jnp.broadcast_to(place, (vecs, slots)).astype(bf16)
        place = jnp.dot(place, spread, preferred_element_type=f32)
        keys[k] = jnp.where(same, place, -1.0)

    down = lax.broadcasted_iota(i32, (tile, tile), 0)
    over = lax.broadcasted_iota(i32, (tile, tile), 1)
    tri[0] = (down <= over).astype(f32).astype(bf16)
    tri[1] = (down < over).astype(f32).astype(bf16)

    def split_group(g, _):
        tile_copy(g).wait()
        for i in range(GROUP):
            s = g * GROUP + i
            gap = jnp.full((1, tile), coords[0, 0, 0, s] - coords[1, 0, 0, s], i32)
            off = jnp.minimum(gap * gap, 1).astype(f32).astype(bf16)
            stored = lower[s]
            upper[s] = stored * jnp.maximum(tri[0], off)
            lower[s] = stored * jnp.maximum(tri[1], off)
        return 0

    lax.fori_loop(0, groups, split_group, 0)

    for d in (2, 1, 3):
        slot = 2 * ((chip + 4 - d) % 4) + core
        chip_copy(d, slot).wait_recv()
        fwd_copy(d, slot).start()
    sib_copy(sib).wait_recv()
    own_c.wait()
    for d in (2, 1, 3):
        fwd_copy(d, 2 * ((chip + 4 - d) % 4) + 1 - core).wait_recv()

    def forward_group(g, _):
        outs = []
        for i in range(GROUP):
            s = g * GROUP + i
            col = coords[1, 0, 0, s]
            at = lax.div(col, span) * per_slab + lax.rem(col, per_slab)
            outs.append(
                lax.dot_general(
                    xc[at], upper[s], (((1,), (1,)), ((), ())),
                    preferred_element_type=f32,
                ).astype(bf16)
            )
        rows = pl.ds(pl.multiple_of(g * GROUP * vecs, GROUP * vecs), GROUP * vecs)
        made[rows, :] = jnp.concatenate(outs, axis=0)
        return 0

    def mirror_group(g, _):
        outs = []
        for i in range(GROUP):
            s = g * GROUP + i
            row = lax.rem(coords[0, 0, 0, s], span)
            outs.append(
                jnp.dot(xr[row], lower[s], preferred_element_type=f32).astype(bf16)
            )
        rows = pl.ds(pl.multiple_of(g * GROUP * vecs, GROUP * vecs), GROUP * vecs)
        made[rows, :] = jnp.concatenate(outs, axis=0)
        return 0

    def combine(k, owner, dst):
        def pick(p, _):
            rows = pl.ds(pl.multiple_of(p * vecs, vecs), vecs)
            wanted = (owner * per_slab + p).astype(f32)
            onehot[rows, :] = jnp.where(keys[k] == wanted, 1.0, 0.0).astype(bf16)
            return 0

        lax.fori_loop(0, per_slab, pick, 0, unroll=4)
        dst[owner] = jnp.dot(onehot[...], made[...], preferred_element_type=f32).astype(bf16)

    def add(dst, a, b):
        dst[...] = (a[...].astype(f32) + b[...].astype(f32)).astype(dst.dtype)

    def chain(at_right, d, at_left, e):
        @pl.when(c == at_right)
        def _():
            right(d, r_out.at[d]).wait_recv()
            add(r_out.at[d], f_ref.at[d], r_in.at[d])
            right(d, r_out.at[d]).start()

        @pl.when(c == at_left)
        def _():
            left(e, l_out.at[e]).wait_recv()
            add(l_out.at[e], f_ref.at[e], l_in.at[e])
            left(e, l_out.at[e]).start()

    lax.fori_loop(0, groups, forward_group, 0)

    half = c // 2
    for i in range(4):
        combine(0, (3 - i) * (1 - half) + i * half, f_ref)
        if i == 3:
            break

        @pl.when(c == 0)
        def _():
            right(3 - i, f_ref.at[3 - i]).start()

        @pl.when(c == 3)
        def _():
            left(i, f_ref.at[i]).start()

    own_r.wait()
    for d in (2, 1, 3):
        z_copy(d, (c + 4 - d) % 4).wait_recv()
    lax.fori_loop(0, groups, mirror_group, 0)
    chain(1, 3, 2, 0)

    def combine_theirs(j, _):
        combine(1, 2 * ((chip + 1 + j) % 4) + 1 - core, m_ref)
        to_sib((1 + j) % 4).start()
        return 0

    lax.fori_loop(0, 4, combine_theirs, 0)

    for d in (1, 2, 3):
        combine(1, 2 * chip_at(d) + core, m_ref)
        to_sib(d).wait_recv()
        add(chip_out.at[d], m_ref.at[2 * chip_at(d) + core], from_sib.at[d])
        to_chip(d).start()
        if d == 1:
            chain(1, 2, 2, 1)
    chain(2, 3, 1, 0)
    combine(1, r, m_ref)
    to_sib(0).wait_recv()
    for d in (1, 2, 3):
        to_chip(d).wait_recv()

    def rows_of(p):
        rows = pl.ds(pl.multiple_of(p * vecs, vecs), vecs)
        return rows, pl.ds(pl.multiple_of(p * tile, tile), tile)

    def total(p, _):
        rows, at = rows_of(p)
        out = f_ref[c, rows, :].astype(f32) + m_ref[r, rows, :].astype(f32)
        out = out + from_sib[0, rows, :].astype(f32)
        for d in (1, 2, 3):
            out = out + chip_in[d, rows, :].astype(f32)
        o_ref[:, at] = out
        return 0

    lax.fori_loop(0, per_slab, total, 0, unroll=4)

    def last(src):
        def body(p, _):
            rows, at = rows_of(p)
            o_ref[:, at] = o_ref[:, at] + src[c, rows, :].astype(f32)
            return 0

        lax.fori_loop(0, per_slab, body, 0, unroll=4)

    @pl.when(c > 0)
    def _():
        right(c, r_out.at[c]).wait_recv()
        last(r_in)

    @pl.when(c < 3)
    def _():
        left(c, l_out.at[c]).wait_recv()
        last(l_in)

    for d in (1, 2, 3):
        z_copy(d, c).wait_send()
        chip_copy(d, r).wait_send()
        fwd_copy(d, 2 * ((chip + 4 - d) % 4) + core).wait_send()
        to_chip(d).wait_send()
    sib_copy(r).wait_send()
    for d in range(4):
        to_sib(d).wait_send()
    for i in range(3):

        @pl.when(c < 3 - i)
        def _():
            right(3 - i, r_out.at[3 - i]).wait_send()

        @pl.when(c > i)
        def _():
            left(i, l_out.at[i]).wait_send()


def fused(tiles, tile_coords, tile_counts, x):
    slots, tile = tiles.shape[2], tiles.shape[-1]
    vecs, width = x.shape
    slab = width // tile
    rows = slab * vecs
    dma, bf16 = pltpu.SemaphoreType.DMA, jnp.bfloat16
    block = pltpu.VMEM((4, rows, tile), bf16)
    return pl.pallas_call(
        fused_kernel,
        out_shape=jax.ShapeDtypeStruct(x.shape, jnp.float32),
        in_specs=[
            pl.BlockSpec(memory_space=pltpu.SMEM),
            pl.BlockSpec(memory_space=pltpu.SMEM),
            pl.BlockSpec(memory_space=pltpu.VMEM),
            pl.BlockSpec(memory_space=pltpu.VMEM),
            pl.BlockSpec(memory_space=pl.ANY),
        ],
        out_specs=pl.BlockSpec(memory_space=pltpu.VMEM),
        scratch_shapes=[
            pltpu.VMEM((slab, vecs, tile), bf16),
            pltpu.VMEM((4 * slab, vecs, tile), bf16),
            pltpu.VMEM((8 * slab, vecs, tile), bf16),
            pltpu.VMEM((slots, tile, tile), bf16),
            pltpu.VMEM((slots, tile, tile), bf16),
            pltpu.VMEM((2, tile, tile), bf16),
            pltpu.VMEM((slots * vecs, tile), bf16),
            pltpu.VMEM((2, vecs, slots * vecs), jnp.float32),
            pltpu.VMEM((rows, slots * vecs), bf16),
            block,
            pltpu.VMEM((8, rows, tile), bf16),
            *[block] * 7,
            dma((slots // GROUP,)),
            dma((2,)),
            *[dma((4,))] * 4,
            *[dma] * 2,
            *[dma((4,))] * 10,
        ],
        compiler_params=pltpu.CompilerParams(
            collective_id=0, has_side_effects=True, vmem_limit_bytes=VMEM_LIMIT
        ),
        name="fused_product",
    )(tile_coords, tile_counts, tile_coords, x, tiles)


def apply_kernel(
    slots, tile, per_slab, n_cols, coords, count,
    t_ref, xr_ref, xc_ref, f_ref, m_ref, facc, macc,
):
    step = pl.program_id(0)
    group = t_ref.shape[2]

    @pl.when(step == 0)
    def _():
        facc[...] = jnp.zeros_like(facc)
        macc[...] = jnp.zeros_like(macc)

    def place(s):
        tile_row, tile_col = coords[s], coords[slots + s]
        local = tile_row % (per_slab * n_cols)
        row_at = (local // per_slab, pl.multiple_of(local % per_slab * tile, tile))
        col_at = (
            tile_col // (per_slab * n_cols), pl.multiple_of(tile_col % per_slab * tile, tile),
        )
        return row_at, col_at

    def run(masked):
        made = []
        for g in range(group):
            s = step * group + g
            (ro, rp), (co, cp) = place(s)
            x_row = xr_ref[ro, :, pl.ds(rp, tile)]
            x_col = xc_ref[co, :, pl.ds(cp, tile)]
            upper = lower = t_ref[0, 0, g]
            if masked:
                off = coords[s] != coords[slots + s]
                down = lax.broadcasted_iota(jnp.int32, (tile, tile), 0)
                down = jnp.where(off, -1, down)
                across = lax.broadcasted_iota(jnp.int32, (tile, tile), 1)
                stored = upper.astype(jnp.float32)
                upper = jnp.where(down <= across, stored, 0.0).astype(jnp.bfloat16)
                lower = jnp.where(down < across, stored, 0.0).astype(jnp.bfloat16)
            forward = lax.dot_general(
                x_col, upper, (((1,), (1,)), ((), ())), preferred_element_type=jnp.float32
            )
            mirror = lax.dot_general(
                x_row, lower, (((1,), (0,)), ((), ())), preferred_element_type=jnp.float32
            )
            if masked:
                live = s < count[0]
                forward = jnp.where(live, forward, 0.0)
                mirror = jnp.where(live, mirror, 0.0)
            made.append((forward, mirror))
        for g in range(group):
            (ro, rp), (co, cp) = place(step * group + g)
            forward, mirror = made[g]
            facc[ro, :, pl.ds(rp, tile)] += forward
            macc[co, :, pl.ds(cp, tile)] += mirror

    special = coords[step * group] == coords[slots + step * group]
    for g in range(1, group):
        s = step * group + g
        special = special | (coords[s] == coords[slots + s])
    special = special | (step * group + group > count[0])

    @pl.when(special)
    def _():
        run(True)

    @pl.when(jnp.logical_not(special))
    def _():
        run(False)

    @pl.when(step == pl.num_programs(0) - 1)
    def _():
        f_ref[...] = facc[...].astype(f_ref.dtype)
        m_ref[...] = macc[...].astype(m_ref.dtype)


def apply_tiles(tiles, coords, count, xr, xc, tile):
    slots = tiles.shape[2]
    group = GROUP if slots % GROUP == 0 else 1
    n_cols = xr.shape[0]
    per_slab = xr.shape[2] // tile
    whole = lambda a: pl.BlockSpec(a.shape, lambda i, *_: (0, 0, 0))
    return pl.pallas_call(
        functools.partial(apply_kernel, slots, tile, per_slab, n_cols),
        out_shape=(
            jax.ShapeDtypeStruct(xr.shape, jnp.bfloat16),
            jax.ShapeDtypeStruct(xc.shape, jnp.bfloat16),
        ),
        grid_spec=pltpu.PrefetchScalarGridSpec(
            num_scalar_prefetch=2,
            grid=(slots // group,),
            in_specs=[
                pl.BlockSpec((1, 1, group, tile, tile), lambda i, *_: (0, 0, i, 0, 0)),
                whole(xr),
                whole(xc),
            ],
            out_specs=(whole(xr), whole(xc)),
            scratch_shapes=[
                pltpu.VMEM(xr.shape, jnp.float32),
                pltpu.VMEM(xc.shape, jnp.float32),
            ],
        ),
        compiler_params=pltpu.CompilerParams(vmem_limit_bytes=VMEM_LIMIT),
        name="apply_tiles",
    )(coords, count, tiles, xr, xc)


def shards(n_rows, n_cols, tiles, tile_coords, tile_counts, vectors):
    tile = tiles.shape[-1]
    x = vectors.T
    if (n_rows, n_cols) == (8, 4):
        return fused(tiles, tile_coords, tile_counts, x).T
    coords, count = tile_coords.reshape(-1), tile_counts.reshape(-1)
    xr = lax.all_gather(x, "col", axis=0)
    xc = lax.all_gather(x, "row", axis=0)
    f, m = apply_tiles(tiles, coords, count, xr, xc, tile)
    f = lax.all_to_all(f, "col", 0, 0, tiled=True)
    m = lax.all_to_all(m, "row", 0, 0, tiled=True)
    return (jnp.sum(f.astype(jnp.float32), 0) + jnp.sum(m.astype(jnp.float32), 0)).T


def solution(mesh):
    in_specs = (
        P("row", "col", None, None, None),
        P(None, "row", "col", None),
        P("row", "col"),
        P(("row", "col"), None),
    )
    out_specs = P(("row", "col"), None)
    body = functools.partial(shards, mesh.shape["row"], mesh.shape["col"])
    return jax.shard_map(body, mesh=mesh, in_specs=in_specs, out_specs=out_specs, check_vma=False)
```

profile of v0, /device:TPU:0, one launch (start us, length us, event | category | flops | bytes accessed | tf_op | source)
XLA Modules:
  0.0 52.8 jit_solution(12007965005509470989)
XLA Ops:
  0.7 0.0 copy-start
  0.7 0.9 %copy-done = bf16[8192,16]{0,1:T(8,128)(2,1)S(1)} copy-done((bf16[8192,16]{0,1:T(8,128)(2,1)S(1)}, bf16[8192,16]{0,1:T(8,128)(2,1)}, u32[]{:S(2)}) %copy-start) | copy-done | bytes 262168
  1.6 0.0 copy-start.1
  1.6 0.7 %copy-done.1 = s32[2,1,1,80]{3,2,1,0:T(1,128)S(1)} copy-done((s32[2,1,1,80]{3,2,1,0:T(1,128)S(1)}, s32[2,1,1,80]{3,2,1,0:T(1,128)}, u32[]{:S(2)}) %copy-start.1) | copy-done | bytes 664
  2.3 49.7 %fused_product.1 = f32[16,8192]{1,0:T(8,128)S(1)} custom-call(s32[2,1,1,80]{3,2,1,0:T(1,128)S(1)} %copy-done.1, s32[1,1]{1,0:T(1,128)S(6)} %copy.6.count, s32[2,1,1,80]{3,2,1,0:T(1,128)S(1)} %copy-done.1, bf16[16,8192]{1,0:T(8,128)(2,1)S(1)} %bitcast.3, bf16[1,1,80,256,256]{4,3,2,1,0:T(8,128)(2,1)} %t_ref.1), custom_call_target="tpu_custom_call" | custom-call | tf_op jit(solution)/shard_map/fused_product/pallas_call | solution.py:297
  52.0 0.8 %copy.7 = f32[8192,16]{0,1:T(8,128)} copy(f32[8192,16]{0,1:T(8,128)S(1)} %bitcast.2) | data formatting | bytes 1048576
Async XLA Ops:
  0.7 1.0 %copy-start = (bf16[8192,16]{0,1:T(8,128)(2,1)S(1)}, bf16[8192,16]{0,1:T(8,128)(2,1)}, u32[]{:S(2)}) copy-start(bf16[8192,16]{0,1:T(8,128)(2,1)} %param.7) | copy-start | bytes 786436
  1.6 0.7 %copy-start.1 = (s32[2,1,1,80]{3,2,1,0:T(1,128)S(1)}, s32[2,1,1,80]{3,2,1,0:T(1,128)}, u32[]{:S(2)}) copy-start(s32[2,1,1,80]{3,2,1,0:T(1,128)} %coords_v.1) | copy-start | bytes 1924
where the time goes:
time: 53.8 us; the launch traced here: 52.8 us
  Pallas kernels  49.7 us (92%)
  local copies, waits for them, and re-layouts  2.42 us (4%)
  between operations  0.67 us (1%)
    pallas_call x1, Pallas kernels, fused(): pl.pallas_call(fused_kernel, out_shape=jax.ShapeDtypeStruct(x.shape, jnp....  49.7 us
    unnamed x5, local copies, waits for them, and re-layouts  2.42 us

commit v1 on v0

v1 whole, which is shorter than its diff:
```python
import functools

import jax
import jax.numpy as jnp
from jax import lax
from jax.experimental import pallas as pl
from jax.experimental.pallas import tpu as pltpu
from jax.sharding import PartitionSpec as P

MESH = pl.DeviceIdType.MESH
VMEM_LIMIT = 48 * 1024 * 1024
GROUP = 8


def fused_kernel(
    coords_hbm, count_hbm, x_hbm, t_ref, o_ref,
    xv, xr, xc, upper, lower, tri, made, cum_f, cum_m, table_v,
    z_out, z_in, sib_out, sib_in, diag_out, diag_in, near_out, near_in,
    coords, coords_v, count_v, table,
    in_sem, tile_sem, zs, zr, ys, yr, ss, sr, ps, pr, bs, br, ds, dr, ns, nr,
):
    r, c = lax.axis_index("row"), lax.axis_index("col")
    chip, core = r // 2, r % 2
    cx, cy = chip % 2, chip // 2
    beside, across, opposite = 2 * cy + 1 - cx, 2 * (1 - cy) + cx, 3 - chip
    sib = 2 * chip + 1 - core
    xn, yn, dn = 2 * beside + core, 2 * across + core, 2 * opposite + core
    mid = (c == 1) | (c == 2)
    end = (c == 0) | (c == 3)
    next_mid = 1 + c // 3
    near_end, far_mid = 3 * (c - 1), 3 - c
    far_end = 3 - near_end
    slots, tile = upper.shape[0], upper.shape[1]
    vecs = x_hbm.shape[0]
    per_slab = x_hbm.shape[1] // tile
    half = per_slab // 2
    groups = slots // GROUP
    span = 4 * per_slab
    f32, bf16, i32 = jnp.float32, jnp.bfloat16, jnp.int32

    def part(k):
        return pl.ds(k * half, half)

    x_copy = pltpu.make_async_copy(x_hbm, xv, in_sem.at[0])
    coords_copy = pltpu.make_async_copy(coords_hbm, coords, in_sem.at[1])
    coords_v_copy = pltpu.make_async_copy(coords_hbm, coords_v, in_sem.at[2])
    count_copy = pltpu.make_async_copy(count_hbm, count_v, in_sem.at[3])
    table_copy = pltpu.make_async_copy(table_v, table, in_sem.at[4])
    for copy in (x_copy, coords_v_copy, count_copy, coords_copy):
        copy.start()

    def tile_copy(g):
        at = pl.ds(g * GROUP, GROUP)
        return pltpu.make_async_copy(t_ref.at[0, 0, at], lower.at[at], tile_sem.at[g])

    barrier = pltpu.get_barrier_semaphore()
    for row in (xn, yn, sib):
        pl.semaphore_signal(barrier, inc=1, device_id=(row, c), device_id_type=MESH)

    @pl.when(c > 0)
    def _():
        pl.semaphore_signal(barrier, inc=1, device_id=(r, c - 1), device_id_type=MESH)

    @pl.when(c < 3)
    def _():
        pl.semaphore_signal(barrier, inc=1, device_id=(r, c + 1), device_id_type=MESH)

    def start_tiles(g, _):
        tile_copy(g).start()
        return 0

    x_copy.wait()
    lax.fori_loop(0, groups, start_tiles, 0)
    for p in range(per_slab):
        xr[c, p] = xv[:, p * tile : (p + 1) * tile]

    @pl.when(mid)
    def _():
        pl.semaphore_wait(barrier, 5)

    @pl.when(end)
    def _():
        pl.semaphore_wait(barrier, 4)

    def remote(src, dst, send, recv, row, col):
        return pltpu.make_async_remote_copy(
            src, dst, send, recv, device_id=(row, col), device_id_type=MESH
        )

    def z_copy(j, owner, k, to):
        block = xr.at[owner, part(k)]
        return remote(block, block, zs.at[j, k], zr.at[owner, k], r, to)

    def link_half(link, first):
        return (0 if first else 1) if link == 0 else (1 if first else 0)

    links = (xn, yn)

    def own_copy(link, owner, i):
        k = link_half(link, i == 0)
        return remote(
            xr.at[c, part(k)], xc.at[owner, part(k)], ys.at[link, i], yr.at[link, i],
            links[link], c,
        )

    def pass_copy(link, owner):
        k = link_half(link, False)
        block = xc.at[owner, part(k)]
        return remote(block, block, ys.at[link, 2], yr.at[link, 2], links[link], c)

    def sib_copy(i, src, owner, k):
        return remote(src, xc.at[owner, part(k)], ss.at[i, k], sr.at[i, k], sib, c)

    def start_own(k):
        @pl.when(c < 3)
        def _():
            z_copy(0, c, k, c + 1).start()

        @pl.when(c > 0)
        def _():
            z_copy(1, c, k, c - 1).start()

        for link in range(2):
            own_copy(link, r, k).start()

    start_own(0)
    start_own(1)
    for k in range(2):
        sib_copy(0, xr.at[c, part(k)], r, k).start()
    for p in range(per_slab):
        xc[r, p] = xv[:, p * tile : (p + 1) * tile]

    coords_v_copy.wait()
    count_copy.wait()
    rows_v, cols_v = coords_v[0, 0], coords_v[1, 0]
    lane = lax.broadcasted_iota(i32, (slots, slots), 1)
    down = lax.broadcasted_iota(i32, (slots, slots), 0)
    live = lax.broadcasted_iota(i32, (1, slots), 1) < count_v[0:1, 0:1]
    places = (rows_v % span, cols_v // span * per_slab + cols_v % per_slab)
    width = table_v.shape[1]
    order = lax.broadcasted_iota(i32, (slots, width), 0) + 1
    target = lax.broadcasted_iota(i32, (slots, width), 1)
    for k in range(2):
        place = jnp.where(live, places[k], -1)
        tall = jnp.where(down == lane, jnp.broadcast_to(place, (slots, slots)), 0)
        tall = jnp.sum(tall.astype(f32), axis=1, keepdims=True).astype(i32)
        before = jnp.where((tall == place) & (down < lane), down + 1, 0)
        table_v[2 * k : 2 * k + 1, 0:slots] = jnp.max(before, axis=0, keepdims=True)
        found = jnp.where(tall == target, order, 0)
        table_v[2 * k + 1 : 2 * k + 2, :] = jnp.max(found, axis=0, keepdims=True)
    table_copy.start()
    cum_f[0] = jnp.zeros(cum_f.shape[1:], f32)
    cum_m[0] = jnp.zeros(cum_m.shape[1:], f32)

    down = lax.broadcasted_iota(i32, (tile, tile), 0)
    over = lax.broadcasted_iota(i32, (tile, tile), 1)
    tri[0] = (down <= over).astype(f32).astype(bf16)
    tri[1] = (down < over).astype(f32).astype(bf16)
    coords_copy.wait()

    def split_group(g, _):
        tile_copy(g).wait()
        for i in range(GROUP):
            s = g * GROUP + i
            gap = jnp.full((1, tile), coords[0, 0, 0, s] - coords[1, 0, 0, s], i32)
            off = jnp.minimum(gap * gap, 1).astype(f32).astype(bf16)
            stored = lower[s]
            upper[s] = stored * jnp.maximum(tri[0], off)
            lower[s] = stored * jnp.maximum(tri[1], off)
        return 0

    def split(a, b):
        lax.fori_loop(a * groups // 10, b * groups // 10, split_group, 0)

    def z_pass_one(k):
        @pl.when(mid)
        def _():
            z_copy(2, c - 1, k, c + 1).wait_recv()
            z_copy(2, c - 1, k, c + 1).start()
            z_copy(3, c + 1, k, c - 1).wait_recv()
            z_copy(3, c + 1, k, c - 1).start()

    def z_pass_two(k):
        @pl.when(mid)
        def _():
            z_copy(4, far_end, k, near_end).wait_recv()
            z_copy(4, far_end, k, near_end).start()

    split(0, 2)
    for link in range(2):
        own_copy(link, links[link], 0).wait_recv()
        pass_copy(1 - link, links[link]).start()
        k = link_half(link, True)
        sib_copy(1 + link, xc.at[links[link], part(k)], links[link], k).start()
    z_pass_one(0)
    split(2, 5)
    for link in range(2):
        own_copy(link, links[link], 1).wait_recv()
        k = link_half(link, False)
        sib_copy(1 + link, xc.at[links[link], part(k)], links[link], k).start()
    z_pass_one(1)
    split(5, 8)
    z_pass_two(0)
    split(8, 10)
    for link in range(2):
        pass_copy(link, dn).wait_recv()
        k = link_half(link, False)
        sib_copy(3, xc.at[dn, part(k)], dn, k).start()
    z_pass_two(1)
    table_copy.wait()
    for i, owner in enumerate((sib, 2 * beside + 1 - core, 2 * across + 1 - core,
                               2 * opposite + 1 - core)):
        for k in range(2):
            sib_copy(i, xc.at[owner, part(k)], owner, k).wait_recv()

    def running_sums(make, cum, at):
        def link(g):
            for i in range(GROUP):
                s = g * GROUP + i
                cum[s + 1] = made[s] + cum[table[at, s]]

        def group(g, _):
            for i in range(GROUP):
                make(g * GROUP + i)
            link(g - 1)
            return 0

        for i in range(GROUP):
            make(i)
        lax.fori_loop(1, groups, group, 0)
        link(groups - 1)

    def forward(s):
        col = coords[1, 0, 0, s]
        at = lax.div(col, span) * per_slab + lax.rem(col, per_slab)
        made[s] = lax.dot_general(
            xc[lax.div(at, per_slab), lax.rem(at, per_slab)], upper[s],
            (((1,), (1,)), ((), ())), preferred_element_type=f32,
        )

    def mirror(s):
        row = lax.rem(coords[0, 0, 0, s], span)
        made[s] = jnp.dot(
            xr[lax.div(row, per_slab), lax.rem(row, per_slab)], lower[s],
            preferred_element_type=f32,
        )

    def fill(dst, cum, at, owner, k, *more, to=None):
        base = k * half

        def body(i, _):
            out = cum[table[at, owner * per_slab + base + i]]
            for source, offset in more:
                out = out + source[offset + i].astype(f32)
            dst[(base if to is None else to) + i] = out.astype(dst.dtype)
            return 0

        lax.fori_loop(0, half, body, 0, unroll=8)

    def near(i, k):
        return remote(
            z_out.at[i, part(k)], z_in.at[i, part(k)], ps.at[i, k], pr.at[i, k], r, next_mid
        )

    def far(i, k):
        return remote(
            z_out.at[i, part(k)], z_in.at[3 + i, part(k)], ps.at[i, k], pr.at[3 + i, k],
            r, far_mid,
        )

    def to_end(k):
        return remote(
            z_out.at[2, part(k)], z_in.at[0, part(k)], ps.at[2, k], pr.at[0, k], r, near_end
        )

    def chain_far(i, k):
        @pl.when(mid)
        def _():
            near(i, k).wait_recv()
            owner = far_end if i == 0 else far_mid
            fill(z_out.at[i], cum_f, 1, owner, k, (z_in.at[i], k * half))
            far(i, k).start()

    def chain_end(k):
        @pl.when(mid)
        def _():
            far(0, k).wait_recv()
            fill(z_out.at[2], cum_f, 1, near_end, k, (z_in.at[3], k * half))
            to_end(k).start()

    def to_sib(j):
        return remote(sib_out.at[j], sib_in.at[j], bs.at[j], br.at[j], sib, c)

    def diag(link):
        return remote(
            diag_out.at[link], diag_in.at[link], ds.at[link], dr.at[link], links[link], c
        )

    def beside_copy(link, i):
        k = link_half(link, i == 0)
        return remote(
            near_out.at[link, part(k)], near_in.at[link, part(k)],
            ns.at[link, i], nr.at[link, i], links[link], c,
        )

    running_sums(forward, cum_f, 0)

    @pl.when(end)
    def _():
        for i, owner in enumerate((3 - c, 3 - next_mid, next_mid)):
            for k in range(2):
                fill(z_out.at[i], cum_f, 1, owner, k)
                near(i, k).start()

        def last_blocks(d, _):
            owner = jnp.where(c == 0, d, 3 - d)
            for k in range(2):
                z_copy(0, owner, k, next_mid).wait_recv()
            return 0

        lax.fori_loop(1, 4, last_blocks, 0)

    running_sums(mirror, cum_m, 2)
    for j, to in enumerate((opposite, beside, across, chip)):
        for k in range(2):
            fill(sib_out.at[j], cum_m, 3, 2 * to + 1 - core, k)
        to_sib(j).start()
    chain_far(0, 0)
    to_sib(0).wait_recv()
    for link in range(2):
        fill(diag_out.at[link], cum_m, 3, dn, link, (sib_in.at[0], link * half), to=0)
        diag(link).start()
    for link in range(2):
        to_sib(1 + link).wait_recv()
        k = link_half(link, True)
        fill(near_out.at[link], cum_m, 3, links[link], k, (sib_in.at[1 + link], k * half))
        beside_copy(link, 0).start()
    chain_far(0, 1)
    for link in range(2):
        diag(1 - link).wait_recv()
        k = link_half(link, False)
        fill(
            near_out.at[link], cum_m, 3, links[link], k,
            (sib_in.at[1 + link], k * half), (diag_in.at[1 - link], 0),
        )
        beside_copy(link, 1).start()
    chain_end(0)
    chain_far(1, 0)
    chain_end(1)
    to_sib(3).wait_recv()

    def blocks(body, a, b):
        def step(p, _):
            body(p, pl.ds(pl.multiple_of(p * tile, tile), tile))
            return 0

        lax.fori_loop(a, b, step, 0, unroll=8)

    def base(p, at):
        o_ref[:, at] = (
            cum_f[table[1, c * per_slab + p]] + cum_m[table[3, r * per_slab + p]]
            + sib_in[3, p].astype(f32)
        )

    def add(k, *sources):
        def body(p, at):
            out = o_ref[:, at]
            for source in sources:
                out = out + source[p].astype(f32)
            o_ref[:, at] = out

        blocks(body, k * half, (k + 1) * half)

    blocks(base, 0, per_slab)

    @pl.when(end)
    def _():
        for k in range(2):
            to_end(k).wait_recv()
            add(k, z_in.at[0])

    chain_far(1, 1)
    for link in range(2):
        beside_copy(link, 0).wait_recv()
        add(link_half(link, True), near_in.at[link])
    for link in range(2):
        beside_copy(link, 1).wait_recv()
        add(link_half(link, False), near_in.at[link])

    @pl.when(mid)
    def _():
        for k in range(2):
            far(1, k).wait_recv()
            near(2, k).wait_recv()
            add(k, z_in.at[4], z_in.at[2])

    for k in range(2):

        @pl.when(c < 3)
        def _():
            z_copy(0, c, k, c + 1).wait_send()

        @pl.when(c > 0)
        def _():
            z_copy(1, c, k, c - 1).wait_send()

        @pl.when(mid)
        def _():
            z_copy(2, c - 1, k, c + 1).wait_send()
            z_copy(3, c + 1, k, c - 1).wait_send()
            z_copy(4, far_end, k, near_end).wait_send()

        for i in range(3):
            near(i, k).wait_send()
        for link in range(2):
            own_copy(link, r, k).wait_send()
            beside_copy(link, k).wait_send()
        for i, owner in enumerate((r, xn, yn, dn)):
            sib_copy(i, xc.at[owner, part(k)], owner, k).wait_send()
    for link in range(2):
        pass_copy(link, links[1 - link]).wait_send()
        diag(link).wait_send()
    for j in range(4):
        to_sib(j).wait_send()


def fused(tiles, tile_coords, tile_counts, x):
    slots, tile = tiles.shape[2], tiles.shape[-1]
    vecs, width = x.shape
    slab = width // tile
    half = slab // 2
    dma, bf16, f32, i32 = pltpu.SemaphoreType.DMA, jnp.bfloat16, jnp.float32, jnp.int32

    def blocks(*lead, dtype=bf16):
        return pltpu.VMEM((*lead, vecs, tile), dtype)

    return pl.pallas_call(
        fused_kernel,
        out_shape=jax.ShapeDtypeStruct(x.shape, f32),
        in_specs=[pl.BlockSpec(memory_space=pltpu.HBM)] * 4,
        out_specs=pl.BlockSpec(memory_space=pltpu.VMEM),
        scratch_shapes=[
            pltpu.VMEM(x.shape, bf16),
            blocks(4, slab),
            blocks(8, slab),
            pltpu.VMEM((slots, tile, tile), bf16),
            pltpu.VMEM((slots, tile, tile), bf16),
            pltpu.VMEM((2, tile, tile), bf16),
            blocks(slots, dtype=f32),
            blocks(slots + 1, dtype=f32),
            blocks(slots + 1, dtype=f32),
            pltpu.VMEM((8, 8 * slab), i32),
            blocks(3, slab),
            blocks(5, slab),
            blocks(4, slab),
            blocks(4, slab),
            blocks(2, half),
            blocks(2, half),
            blocks(2, slab),
            blocks(2, slab),
            pltpu.SMEM(tile_coords.shape, i32),
            pltpu.VMEM(tile_coords.shape, i32),
            pltpu.VMEM((1, 1), i32),
            pltpu.SMEM((8, 8 * slab), i32),
            dma((5,)),
            dma((slots // GROUP,)),
            dma((5, 2)), dma((4, 2)),
            dma((2, 3)), dma((2, 3)),
            dma((4, 2)), dma((4, 2)),
            dma((3, 2)), dma((5, 2)),
            dma((4,)), dma((4,)),
            dma((2,)), dma((2,)),
            dma((2, 2)), dma((2, 2)),
        ],
        compiler_params=pltpu.CompilerParams(
            collective_id=0, has_side_effects=True, vmem_limit_bytes=VMEM_LIMIT
        ),
        name="fused_product",
    )(tile_coords, tile_counts, x, tiles)


def apply_kernel(
    slots, tile, per_slab, n_cols, coords, count,
    t_ref, xr_ref, xc_ref, f_ref, m_ref, facc, macc,
):
    step = pl.program_id(0)
    group = t_ref.shape[2]

    @pl.when(step == 0)
    def _():
        facc[...] = jnp.zeros_like(facc)
        macc[...] = jnp.zeros_like(macc)

    def place(s):
        tile_row, tile_col = coords[s], coords[slots + s]
        local = tile_row % (per_slab * n_cols)
        row_at = (local // per_slab, pl.multiple_of(local % per_slab * tile, tile))
        col_at = (
            tile_col // (per_slab * n_cols), pl.multiple_of(tile_col % per_slab * tile, tile),
        )
        return row_at, col_at

    def run(masked):
        made = []
        for g in range(group):
            s = step * group + g
            (ro, rp), (co, cp) = place(s)
            x_row = xr_ref[ro, :, pl.ds(rp, tile)]
            x_col = xc_ref[co, :, pl.ds(cp, tile)]
            upper = lower = t_ref[0, 0, g]
            if masked:
                off = coords[s] != coords[slots + s]
                down = lax.broadcasted_iota(jnp.int32, (tile, tile), 0)
                down = jnp.where(off, -1, down)
                across = lax.broadcasted_iota(jnp.int32, (tile, tile), 1)
                stored = upper.astype(jnp.float32)
                upper = jnp.where(down <= across, stored, 0.0).astype(jnp.bfloat16)
                lower = jnp.where(down < across, stored, 0.0).astype(jnp.bfloat16)
            forward = lax.dot_general(
                x_col, upper, (((1,), (1,)), ((), ())), preferred_element_type=jnp.float32
            )
            mirror = lax.dot_general(
                x_row, lower, (((1,), (0,)), ((), ())), preferred_element_type=jnp.float32
            )
            if masked:
                live = s < count[0]
                forward = jnp.where(live, forward, 0.0)
                mirror = jnp.where(live, mirror, 0.0)
            made.append((forward, mirror))
        for g in range(group):
            (ro, rp), (co, cp) = place(step * group + g)
            forward, mirror = made[g]
            facc[ro, :, pl.ds(rp, tile)] += forward
            macc[co, :, pl.ds(cp, tile)] += mirror

    special = coords[step * group] == coords[slots + step * group]
    for g in range(1, group):
        s = step * group + g
        special = special | (coords[s] == coords[slots + s])
    special = special | (step * group + group > count[0])

    @pl.when(special)
    def _():
        run(True)

    @pl.when(jnp.logical_not(special))
    def _():
        run(False)

    @pl.when(step == pl.num_programs(0) - 1)
    def _():
        f_ref[...] = facc[...].astype(f_ref.dtype)
        m_ref[...] = macc[...].astype(m_ref.dtype)


def apply_tiles(tiles, coords, count, xr, xc, tile):
    slots = tiles.shape[2]
    group = GROUP if slots % GROUP == 0 else 1
    n_cols = xr.shape[0]
    per_slab = xr.shape[2] // tile
    whole = lambda a: pl.BlockSpec(a.shape, lambda i, *_: (0, 0, 0))
    return pl.pallas_call(
        functools.partial(apply_kernel, slots, tile, per_slab, n_cols),
        out_shape=(
            jax.ShapeDtypeStruct(xr.shape, jnp.bfloat16),
            jax.ShapeDtypeStruct(xc.shape, jnp.bfloat16),
        ),
        grid_spec=pltpu.PrefetchScalarGridSpec(
            num_scalar_prefetch=2,
            grid=(slots // group,),
            in_specs=[
                pl.BlockSpec((1, 1, group, tile, tile), lambda i, *_: (0, 0, i, 0, 0)),
                whole(xr),
                whole(xc),
            ],
            out_specs=(whole(xr), whole(xc)),
            scratch_shapes=[
                pltpu.VMEM(xr.shape, jnp.float32),
                pltpu.VMEM(xc.shape, jnp.float32),
            ],
        ),
        compiler_params=pltpu.CompilerParams(vmem_limit_bytes=VMEM_LIMIT),
        name="apply_tiles",
    )(coords, count, tiles, xr, xc)


def shards(n_rows, n_cols, tiles, tile_coords, tile_counts, vectors):
    tile = tiles.shape[-1]
    x = vectors.T
    if (n_rows, n_cols) == (8, 4):
        return fused(tiles, tile_coords, tile_counts, x).T
    coords, count = tile_coords.reshape(-1), tile_counts.reshape(-1)
    xr = lax.all_gather(x, "col", axis=0)
    xc = lax.all_gather(x, "row", axis=0)
    f, m = apply_tiles(tiles, coords, count, xr, xc, tile)
    f = lax.all_to_all(f, "col", 0, 0, tiled=True)
    m = lax.all_to_all(m, "row", 0, 0, tiled=True)
    return (jnp.sum(f.astype(jnp.float32), 0) + jnp.sum(m.astype(jnp.float32), 0)).T


def solution(mesh):
    in_specs = (
        P("row", "col", None, None, None),
        P(None, "row", "col", None),
        P("row", "col"),
        P(("row", "col"), None),
    )
    out_specs = P(("row", "col"), None)
    body = functools.partial(shards, mesh.shape["row"], mesh.shape["col"])
    return jax.shard_map(body, mesh=mesh, in_specs=in_specs, out_specs=out_specs, check_vma=False)
```

time: 53.8 us -> 42.8 us (0.80); the launches traced: 52.8 us -> 42.6 us
  Pallas kernels: 49.7 us -> 39.5 us
    pallas_call x1, Pallas kernels: 49.7 us -> 39.5 us  [fused(): pl.pallas_call(fused_kernel, out_shape=jax.ShapeDtypeStruct(x.shape, f32)...]
where the time goes in v1:
time: 42.8 us; the launch traced here: 42.6 us
  Pallas kernels  39.5 us (92%)
  local copies, waits for them, and re-layouts  2.42 us (6%)
  between operations  0.67 us (2%)
    pallas_call x1, Pallas kernels, fused(): pl.pallas_call(fused_kernel, out_shape=jax.ShapeDtypeStruct(x.shape, f32)...  39.5 us
    unnamed x5, local copies, waits for them, and re-layouts  2.42 us

profile of v1, /device:TPU:0, one launch (start us, length us, event | category | flops | bytes accessed | tf_op | source)
XLA Modules:
  0.0 42.6 jit_solution(7465557454921382239)
XLA Ops:
  0.7 0.0 copy-start
  0.7 0.9 %copy-done = bf16[8192,16]{0,1:T(8,128)(2,1)S(1)} copy-done((bf16[8192,16]{0,1:T(8,128)(2,1)S(1)}, bf16[8192,16]{0,1:T(8,128)(2,1)}, u32[]{:S(2)}) %copy-start) | copy-done | bytes 262168
  1.6 0.0 copy-start.1
  1.6 0.7 %copy-done.1 = s32[2,1,1,80]{3,2,1,0:T(1,128)S(1)} copy-done((s32[2,1,1,80]{3,2,1,0:T(1,128)S(1)}, s32[2,1,1,80]{3,2,1,0:T(1,128)}, u32[]{:S(2)}) %copy-start.1) | copy-done | bytes 664
  2.3 39.5 %fused_product.1 = f32[16,8192]{1,0:T(8,128)S(1)} custom-call(s32[2,1,1,80]{3,2,1,0:T(1,128)S(1)} %copy-done.1, s32[1,1]{1,0:T(1,128)S(6)} %copy.6.count_hbm, bf16[16,8192]{1,0:T(8,128)(2,1)S(1)} %bitcast.3, bf16[1,1,80,256,256]{4,3,2,1,0:T(8,128)(2,1)} %t_ref.1), custom_call_target="tpu_custom_call" | custom-call | tf_op jit(solution)/shard_map/fused_product/pallas_call | solution.py:437
  41.8 0.8 %copy.7 = f32[8192,16]{0,1:T(8,128)} copy(f32[8192,16]{0,1:T(8,128)S(1)} %bitcast.2) | data formatting | bytes 1048576
Async XLA Ops:
  0.7 1.0 %copy-start = (bf16[8192,16]{0,1:T(8,128)(2,1)S(1)}, bf16[8192,16]{0,1:T(8,128)(2,1)}, u32[]{:S(2)}) copy-start(bf16[8192,16]{0,1:T(8,128)(2,1)} %param.7) | copy-start | bytes 786436
  1.6 0.7 %copy-start.1 = (s32[2,1,1,80]{3,2,1,0:T(1,128)S(1)}, s32[2,1,1,80]{3,2,1,0:T(1,128)}, u32[]{:S(2)}) copy-start(s32[2,1,1,80]{3,2,1,0:T(1,128)} %coords_hbm.1) | copy-start | bytes 1924

commit v2 on v1

--- a/solution.py
+++ b/solution.py
@@ -10,6 +10,7 @@
 MESH = pl.DeviceIdType.MESH
 VMEM_LIMIT = 48 * 1024 * 1024
 GROUP = 8
+STEP = 40
 
 
 def fused_kernel(
@@ -154,7 +155,7 @@
 
     down = lax.broadcasted_iota(i32, (tile, tile), 0)
     over = lax.broadcasted_iota(i32, (tile, tile), 1)
-    tri[0] = (down <= over).astype(f32).astype(bf16)
+    tri[0] = (down >= over).astype(f32).astype(bf16)
     tri[1] = (down < over).astype(f32).astype(bf16)
     coords_copy.wait()
 
@@ -165,7 +166,7 @@
             gap = jnp.full((1, tile), coords[0, 0, 0, s] - coords[1, 0, 0, s], i32)
             off = jnp.minimum(gap * gap, 1).astype(f32).astype(bf16)
             stored = lower[s]
-            upper[s] = stored * jnp.maximum(tri[0], off)
+            upper[s] = stored.T * jnp.maximum(tri[0], off)
             lower[s] = stored * jnp.maximum(tri[1], off)
         return 0
 
@@ -215,27 +216,27 @@
 
     def running_sums(make, cum, at):
         def link(g):
-            for i in range(GROUP):
-                s = g * GROUP + i
+            for i in range(STEP):
+                s = g * STEP + i
                 cum[s + 1] = made[s] + cum[table[at, s]]
 
         def group(g, _):
-            for i in range(GROUP):
-                make(g * GROUP + i)
+            for i in range(STEP):
+                make(g * STEP + i)
             link(g - 1)
             return 0
 
-        for i in range(GROUP):
+        for i in range(STEP):
             make(i)
-        lax.fori_loop(1, groups, group, 0)
-        link(groups - 1)
+        lax.fori_loop(1, slots // STEP, group, 0)
+        link(slots // STEP - 1)
 
     def forward(s):
         col = coords[1, 0, 0, s]
         at = lax.div(col, span) * per_slab + lax.rem(col, per_slab)
-        made[s] = lax.dot_general(
+        made[s] = jnp.dot(
             xc[lax.div(at, per_slab), lax.rem(at, per_slab)], upper[s],
-            (((1,), (1,)), ((), ())), preferred_element_type=f32,
+            preferred_element_type=f32,
         )
 
     def mirror(s):

time: 42.8 us -> 39.5 us (0.923)
  Pallas kernels: 39.5 us -> 36.3 us
    pallas_call x1, Pallas kernels: 39.5 us -> 36.3 us  [fused(): pl.pallas_call(fused_kernel, out_shape=jax.ShapeDtypeStruct(x.shape, f32)...]
where the time goes in v2:
time: 39.5 us; the launch traced here: 39.4 us
  Pallas kernels  36.3 us (92%)
  local copies, waits for them, and re-layouts  2.42 us (6%)
  between operations  0.67 us (2%)
    pallas_call x1, Pallas kernels, fused(): pl.pallas_call(fused_kernel, out_shape=jax.ShapeDtypeStruct(x.shape, f32)...  36.3 us
    unnamed x5, local copies, waits for them, and re-layouts  2.42 us

profile of v2, /device:TPU:0, one launch (start us, length us, event | category | flops | bytes accessed | tf_op | source)
XLA Modules:
  0.0 39.4 jit_solution(9767813270797924189)
XLA Ops:
  0.7 0.0 copy-start
  0.7 0.9 %copy-done = bf16[8192,16]{0,1:T(8,128)(2,1)S(1)} copy-done((bf16[8192,16]{0,1:T(8,128)(2,1)S(1)}, bf16[8192,16]{0,1:T(8,128)(2,1)}, u32[]{:S(2)}) %copy-start) | copy-done | bytes 262168
  1.6 0.0 copy-start.1
  1.6 0.7 %copy-done.1 = s32[2,1,1,80]{3,2,1,0:T(1,128)S(1)} copy-done((s32[2,1,1,80]{3,2,1,0:T(1,128)S(1)}, s32[2,1,1,80]{3,2,1,0:T(1,128)}, u32[]{:S(2)}) %copy-start.1) | copy-done | bytes 664
  2.3 36.3 %fused_product.1 = f32[16,8192]{1,0:T(8,128)S(1)} custom-call(s32[2,1,1,80]{3,2,1,0:T(1,128)S(1)} %copy-done.1, s32[1,1]{1,0:T(1,128)S(6)} %copy.6.count_hbm, bf16[16,8192]{1,0:T(8,128)(2,1)S(1)} %bitcast.3, bf16[1,1,80,256,256]{4,3,2,1,0:T(8,128)(2,1)} %t_ref.1), custom_call_target="tpu_custom_call" | custom-call | tf_op jit(solution)/shard_map/fused_product/pallas_call | solution.py:438
  38.6 0.8 %copy.7 = f32[8192,16]{0,1:T(8,128)} copy(f32[8192,16]{0,1:T(8,128)S(1)} %bitcast.2) | data formatting | bytes 1048576
Async XLA Ops:
  0.7 1.0 %copy-start = (bf16[8192,16]{0,1:T(8,128)(2,1)S(1)}, bf16[8192,16]{0,1:T(8,128)(2,1)}, u32[]{:S(2)}) copy-start(bf16[8192,16]{0,1:T(8,128)(2,1)} %param.7) | copy-start | bytes 786436
  1.6 0.7 %copy-start.1 = (s32[2,1,1,80]{3,2,1,0:T(1,128)S(1)}, s32[2,1,1,80]{3,2,1,0:T(1,128)}, u32[]{:S(2)}) copy-start(s32[2,1,1,80]{3,2,1,0:T(1,128)} %coords_hbm.1) | copy-start | bytes 1924

commit v3 on v2

--- a/solution.py
+++ b/solution.py
@@ -10,12 +10,14 @@
 MESH = pl.DeviceIdType.MESH
 VMEM_LIMIT = 48 * 1024 * 1024
 GROUP = 8
-STEP = 40
+LAG = 8
+LATE_ROWS = 35
+LATE_COLS = 28
 
 
 def fused_kernel(
     coords_hbm, count_hbm, x_hbm, t_ref, o_ref,
-    xv, xr, xc, upper, lower, tri, made, cum_f, cum_m, table_v,
+    xv, xr, xc, xr_late, xc_late, upper, lower, tri, made, cum_f, cum_m, table_v,
     z_out, z_in, sib_out, sib_in, diag_out, diag_in, near_out, near_in,
     coords, coords_v, count_v, table,
     in_sem, tile_sem, zs, zr, ys, yr, ss, sr, ps, pr, bs, br, ds, dr, ns, nr,
@@ -39,6 +41,9 @@
     span = 4 * per_slab
     f32, bf16, i32 = jnp.float32, jnp.bfloat16, jnp.int32
 
+    late_row = jnp.where(c < 2, 3, 0)
+    late_col = 2 * opposite + 1 - core
+
     def part(k):
         return pl.ds(k * half, half)
 
@@ -88,9 +93,19 @@
             src, dst, send, recv, device_id=(row, col), device_id_type=MESH
         )
 
-    def z_copy(j, owner, k, to):
-        block = xr.at[owner, part(k)]
-        return remote(block, block, zs.at[j, k], zr.at[owner, k], r, to)
+    def z_copy(j, owner, k, to, src=None, dst=None):
+        src = xr.at[owner, part(k)] if src is None else src.at[part(k)]
+        dst = xr.at[owner, part(k)] if dst is None else dst.at[part(k)]
+        return remote(src, dst, zs.at[j, k], zr.at[owner, k], r, to)
+
+    def z_inner(k):
+        return z_copy(2, near_end, k, far_mid, dst=xr_late)
+
+    def z_outer(k):
+        return z_copy(3, far_mid, k, near_end)
+
+    def z_far(k):
+        return z_copy(4, far_end, k, near_end, src=xr_late, dst=xr_late)
 
     def link_half(link, first):
         return (0 if first else 1) if link == 0 else (1 if first else 0)
@@ -110,7 +125,8 @@
         return remote(block, block, ys.at[link, 2], yr.at[link, 2], links[link], c)
 
     def sib_copy(i, src, owner, k):
-        return remote(src, xc.at[owner, part(k)], ss.at[i, k], sr.at[i, k], sib, c)
+        dst = xc_late.at[part(k)] if i == 3 else xc.at[owner, part(k)]
+        return remote(src, dst, ss.at[i, k], sr.at[i, k], sib, c)
 
     def start_own(k):
         @pl.when(c < 3)
@@ -141,10 +157,27 @@
     width = table_v.shape[1]
     order = lax.broadcasted_iota(i32, (slots, width), 0) + 1
     target = lax.broadcasted_iota(i32, (slots, width), 1)
+    lates = (cols_v // span == late_col, rows_v % span // per_slab == late_row)
+
+    def on_rows(values):
+        wide = jnp.where(down == lane, jnp.broadcast_to(values, (slots, slots)), 0)
+        return jnp.sum(wide.astype(f32), axis=1, keepdims=True).astype(i32)
+
+    def count_of(mask):
+        return jnp.sum(jnp.where(mask, 1.0, 0.0), axis=1, keepdims=True).astype(i32)
+
     for k in range(2):
         place = jnp.where(live, places[k], -1)
-        tall = jnp.where(down == lane, jnp.broadcast_to(place, (slots, slots)), 0)
-        tall = jnp.sum(tall.astype(f32), axis=1, keepdims=True).astype(i32)
+        late = jnp.where(live & lates[k], 1, 0)
+        ahead = count_of((late == 0) & (lane < down))
+        behind = count_of((late == 1) & (lane >= down))
+        spot = jnp.where(on_rows(late) == 1, slots - behind, ahead)
+        here = spot == lane
+        table_v[4 + k : 5 + k, 0:slots] = jnp.max(
+            jnp.where(here, down, 0), axis=0, keepdims=True
+        )
+        place = jnp.max(jnp.where(here, on_rows(place) + 1, 0), axis=0, keepdims=True) - 1
+        tall = on_rows(place)
         before = jnp.where((tall == place) & (down < lane), down + 1, 0)
         table_v[2 * k : 2 * k + 1, 0:slots] = jnp.max(before, axis=0, keepdims=True)
         found = jnp.where(tall == target, order, 0)
@@ -155,6 +188,12 @@
 
     down = lax.broadcasted_iota(i32, (tile, tile), 0)
     over = lax.broadcasted_iota(i32, (tile, tile), 1)
+    def clear_late(p, _):
+        xr[late_row, p] = jnp.zeros(xr.shape[2:], bf16)
+        xc[late_col, p] = jnp.zeros(xc.shape[2:], bf16)
+        return 0
+
+    lax.fori_loop(0, per_slab, clear_late, 0)
     tri[0] = (down >= over).astype(f32).astype(bf16)
     tri[1] = (down < over).astype(f32).astype(bf16)
     coords_copy.wait()
@@ -176,16 +215,16 @@
     def z_pass_one(k):
         @pl.when(mid)
         def _():
-            z_copy(2, c - 1, k, c + 1).wait_recv()
-            z_copy(2, c - 1, k, c + 1).start()
-            z_copy(3, c + 1, k, c - 1).wait_recv()
-            z_copy(3, c + 1, k, c - 1).start()
+            z_copy(2, near_end, k, far_mid).wait_recv()
+            z_inner(k).start()
+            z_outer(k).wait_recv()
+            z_outer(k).start()
 
     def z_pass_two(k):
         @pl.when(mid)
         def _():
-            z_copy(4, far_end, k, near_end).wait_recv()
-            z_copy(4, far_end, k, near_end).start()
+            z_far(k).wait_recv()
+            z_far(k).start()
 
     split(0, 2)
     for link in range(2):
@@ -209,39 +248,44 @@
         sib_copy(3, xc.at[dn, part(k)], dn, k).start()
     z_pass_two(1)
     table_copy.wait()
-    for i, owner in enumerate((sib, 2 * beside + 1 - core, 2 * across + 1 - core,
-                               2 * opposite + 1 - core)):
+
+    def sib_wait(i, owner):
         for k in range(2):
             sib_copy(i, xc.at[owner, part(k)], owner, k).wait_recv()
 
-    def running_sums(make, cum, at):
-        def link(g):
-            for i in range(STEP):
-                s = g * STEP + i
-                cum[s + 1] = made[s] + cum[table[at, s]]
-
-        def group(g, _):
-            for i in range(STEP):
-                make(g * STEP + i)
-            link(g - 1)
+    for i, owner in enumerate((sib, 2 * beside + 1 - core, 2 * across + 1 - core)):
+        sib_wait(i, owner)
+
+    def fetch_late(dst, owner, src):
+        def body(p, _):
+            dst[owner, p] = src[p]
             return 0
 
-        for i in range(STEP):
-            make(i)
-        lax.fori_loop(1, slots // STEP, group, 0)
-        link(slots // STEP - 1)
-
-    def forward(s):
+        lax.fori_loop(0, per_slab, body, 0, unroll=8)
+
+    def running_sums(make, cum, at, a, b):
+        def link(n):
+            cum[n + 1] = made[n] + cum[table[at, n]]
+
+        for n in range(a, b):
+            make(n)
+            if n - LAG >= a:
+                link(n - LAG)
+        for n in range(max(a, b - LAG), b):
+            link(n)
+
+    def forward(n):
+        s = table[4, n]
         col = coords[1, 0, 0, s]
-        at = lax.div(col, span) * per_slab + lax.rem(col, per_slab)
-        made[s] = jnp.dot(
-            xc[lax.div(at, per_slab), lax.rem(at, per_slab)], upper[s],
+        made[n] = jnp.dot(
+            xc[lax.div(col, span), lax.rem(col, per_slab)], upper[s],
             preferred_element_type=f32,
         )
 
-    def mirror(s):
+    def mirror(n):
+        s = table[5, n]
         row = lax.rem(coords[0, 0, 0, s], span)
-        made[s] = jnp.dot(
+        made[n] = jnp.dot(
             xr[lax.div(row, per_slab), lax.rem(row, per_slab)], lower[s],
             preferred_element_type=f32,
         )
@@ -304,7 +348,10 @@
             ns.at[link, i], nr.at[link, i], links[link], c,
         )
 
-    running_sums(forward, cum_f, 0)
+    running_sums(forward, cum_f, 0, 0, slots - LATE_COLS)
+    sib_wait(3, late_col)
+    fetch_late(xc, late_col, xc_late)
+    running_sums(forward, cum_f, 0, slots - LATE_COLS, slots)
 
     @pl.when(end)
     def _():
@@ -313,15 +360,21 @@
                 fill(z_out.at[i], cum_f, 1, owner, k)
                 near(i, k).start()
 
-        def last_blocks(d, _):
-            owner = jnp.where(c == 0, d, 3 - d)
+    @pl.when(end)
+    def _():
+        for owner in (next_mid, 3 - next_mid):
             for k in range(2):
                 z_copy(0, owner, k, next_mid).wait_recv()
-            return 0
-
-        lax.fori_loop(1, 4, last_blocks, 0)
-
-    running_sums(mirror, cum_m, 2)
+
+    running_sums(mirror, cum_m, 2, 0, slots - LATE_ROWS)
+
+    @pl.when(end)
+    def _():
+        for k in range(2):
+            z_copy(0, late_row, k, next_mid, dst=xr_late).wait_recv()
+
+    fetch_late(xr, late_row, xr_late)
+    running_sums(mirror, cum_m, 2, slots - LATE_ROWS, slots)
     for j, to in enumerate((opposite, beside, across, chip)):
         for k in range(2):
             fill(sib_out.at[j], cum_m, 3, 2 * to + 1 - core, k)
@@ -407,9 +460,9 @@
 
         @pl.when(mid)
         def _():
-            z_copy(2, c - 1, k, c + 1).wait_send()
-            z_copy(3, c + 1, k, c - 1).wait_send()
-            z_copy(4, far_end, k, near_end).wait_send()
+            z_inner(k).wait_send()
+            z_outer(k).wait_send()
+            z_far(k).wait_send()
 
         for i in range(3):
             near(i, k).wait_send()
@@ -444,6 +497,8 @@
             pltpu.VMEM(x.shape, bf16),
             blocks(4, slab),
             blocks(8, slab),
+            blocks(slab),
+            blocks(slab),
             pltpu.VMEM((slots, tile, tile), bf16),
             pltpu.VMEM((slots, tile, tile), bf16),
             pltpu.VMEM((2, tile, tile), bf16),
@@ -477,7 +532,10 @@
             collective_id=0, has_side_effects=True, vmem_limit_bytes=VMEM_LIMIT
         ),
         name="fused_product",
-    )(tile_coords, tile_counts, x, tiles)
+    )(
+        pltpu.with_memory_space_constraint(tile_coords, pltpu.HBM), tile_counts,
+        pltpu.with_memory_space_constraint(x, pltpu.HBM), tiles,
+    )
 
 
 def apply_kernel(

time: 39.5 us -> 37.7 us (0.954)
  local copies, waits for them, and re-layouts: 2.42 us -> 0.8 us
    unnamed x5 -> x1, local copies, waits for them, and re-layouts: 2.42 us -> 0.8 us
where the time goes in v3:
time: 37.7 us; the launch traced here: 37.6 us
  Pallas kernels  36.2 us (96%)
  local copies, waits for them, and re-layouts  0.8 us (2%)
  between operations  0.66 us (2%)
    pallas_call x1, Pallas kernels, fused(): pl.pallas_call(fused_kernel, out_shape=jax.ShapeDtypeStruct(x.shape, f32)...  36.2 us
    unnamed x1, local copies, waits for them, and re-layouts  0.8 us

profile of v3, /device:TPU:0, one launch (start us, length us, event | category | flops | bytes accessed | tf_op | source)
XLA Modules:
  0.0 37.6 jit_solution(15985568127325783447)
XLA Ops:
  0.7 36.2 %fused_product.1 = f32[16,8192]{1,0:T(8,128)S(1)} custom-call(s32[2,1,1,80]{3,2,1,0:T(1,128)} %coords_hbm.1, s32[1,1]{1,0:T(1,128)S(6)} %copy.6.count_hbm, bf16[16,8192]{1,0:T(8,128)(2,1)} %bitcast.3, bf16[1,1,80,256,256]{4,3,2,1,0:T(8,128)(2,1)} %t_ref.1), custom_call_target="tpu_custom_call" | custom-call | tf_op jit(solution)/shard_map/fused_product/pallas_call | solution.py:491
  36.8 0.8 %copy.7 = f32[8192,16]{0,1:T(8,128)} copy(f32[8192,16]{0,1:T(8,128)S(1)} %bitcast.2) | data formatting | bytes 1048576

commit v4 on v3

--- a/solution.py
+++ b/solution.py
@@ -17,7 +17,7 @@
 
 def fused_kernel(
     coords_hbm, count_hbm, x_hbm, t_ref, o_ref,
-    xv, xr, xc, xr_late, xc_late, upper, lower, tri, made, cum_f, cum_m, table_v,
+    xv, xr, xc, xr_late, xc_late, upper, lower, tri, made, made_m, cum_f, cum_m, table_v,
     z_out, z_in, sib_out, sib_in, diag_out, diag_in, near_out, near_in,
     coords, coords_v, count_v, table,
     in_sem, tile_sem, zs, zr, ys, yr, ss, sr, ps, pr, bs, br, ds, dr, ns, nr,
@@ -37,6 +37,8 @@
     vecs = x_hbm.shape[0]
     per_slab = x_hbm.shape[1] // tile
     half = per_slab // 2
+    pairs, some = per_slab // 2, vecs // 2
+    quarter = pairs // 2
     groups = slots // GROUP
     span = 4 * per_slab
     f32, bf16, i32 = jnp.float32, jnp.bfloat16, jnp.int32
@@ -76,10 +78,8 @@
         return 0
 
     x_copy.wait()
-    lax.fori_loop(0, groups, start_tiles, 0)
     for p in range(per_slab):
-        xr[c, p] = xv[:, p * tile : (p + 1) * tile]
-
+        xc[r, p] = xv[:, p * tile : (p + 1) * tile]
     @pl.when(mid)
     def _():
         pl.semaphore_wait(barrier, 5)
@@ -93,10 +93,10 @@
             src, dst, send, recv, device_id=(row, col), device_id_type=MESH
         )
 
-    def z_copy(j, owner, k, to, src=None, dst=None):
-        src = xr.at[owner, part(k)] if src is None else src.at[part(k)]
-        dst = xr.at[owner, part(k)] if dst is None else dst.at[part(k)]
-        return remote(src, dst, zs.at[j, k], zr.at[owner, k], r, to)
+    def z_copy(j, owner, h, to, src=None, dst=None):
+        src = xr.at[h, owner] if src is None else src.at[h]
+        dst = xr.at[h, owner] if dst is None else dst.at[h]
+        return remote(src, dst, zs.at[j, h], zr.at[owner, h], r, to)
 
     def z_inner(k):
         return z_copy(2, near_end, k, far_mid, dst=xr_late)
@@ -115,7 +115,7 @@
     def own_copy(link, owner, i):
         k = link_half(link, i == 0)
         return remote(
-            xr.at[c, part(k)], xc.at[owner, part(k)], ys.at[link, i], yr.at[link, i],
+            xc.at[r, part(k)], xc.at[owner, part(k)], ys.at[link, i], yr.at[link, i],
             links[link], c,
         )
 
@@ -128,24 +128,28 @@
         dst = xc_late.at[part(k)] if i == 3 else xc.at[owner, part(k)]
         return remote(src, dst, ss.at[i, k], sr.at[i, k], sib, c)
 
-    def start_own(k):
-        @pl.when(c < 3)
-        def _():
-            z_copy(0, c, k, c + 1).start()
-
-        @pl.when(c > 0)
-        def _():
-            z_copy(1, c, k, c - 1).start()
-
+    for k in range(2):
         for link in range(2):
             own_copy(link, r, k).start()
-
-    start_own(0)
-    start_own(1)
+    for p in range(pairs):
+        two = [xv[:, q * tile : (q + 1) * tile].astype(f32) for q in (p, p + pairs)]
+        for h in range(2):
+            rows = [b[h * some : (h + 1) * some] for b in two]
+            xr[h, c, p] = jnp.concatenate(rows, axis=0).astype(bf16)
+
+    for h in range(2):
+
+        @pl.when(c < 3)
+        def _():
+            z_copy(0, c, h, c + 1).start()
+
+        @pl.when(c > 0)
+        def _():
+            z_copy(1, c, h, c - 1).start()
+
+    lax.fori_loop(0, groups, start_tiles, 0)
     for k in range(2):
-        sib_copy(0, xr.at[c, part(k)], r, k).start()
-    for p in range(per_slab):
-        xc[r, p] = xv[:, p * tile : (p + 1) * tile]
+        sib_copy(0, xc.at[r, part(k)], r, k).start()
 
     coords_v_copy.wait()
     count_copy.wait()
@@ -184,13 +188,14 @@
         table_v[2 * k + 1 : 2 * k + 2, :] = jnp.max(found, axis=0, keepdims=True)
     table_copy.start()
     cum_f[0] = jnp.zeros(cum_f.shape[1:], f32)
-    cum_m[0] = jnp.zeros(cum_m.shape[1:], f32)
+    for h in range(2):
+        cum_m[h, 0] = jnp.zeros(cum_m.shape[2:], f32)
 
     down = lax.broadcasted_iota(i32, (tile, tile), 0)
     over = lax.broadcasted_iota(i32, (tile, tile), 1)
     def clear_late(p, _):
-        xr[late_row, p] = jnp.zeros(xr.shape[2:], bf16)
         xc[late_col, p] = jnp.zeros(xc.shape[2:], bf16)
+        xr[p // pairs, late_row, p % pairs] = jnp.zeros(xr.shape[3:], bf16)
         return 0
 
     lax.fori_loop(0, per_slab, clear_late, 0)
@@ -256,17 +261,7 @@
     for i, owner in enumerate((sib, 2 * beside + 1 - core, 2 * across + 1 - core)):
         sib_wait(i, owner)
 
-    def fetch_late(dst, owner, src):
-        def body(p, _):
-            dst[owner, p] = src[p]
-            return 0
-
-        lax.fori_loop(0, per_slab, body, 0, unroll=8)
-
-    def running_sums(make, cum, at, a, b):
-        def link(n):
-            cum[n + 1] = made[n] + cum[table[at, n]]
-
+    def running_sums(make, link, a, b):
         for n in range(a, b):
             make(n)
             if n - LAG >= a:
@@ -274,21 +269,54 @@
         for n in range(max(a, b - LAG), b):
             link(n)
 
-    def forward(n):
-        s = table[4, n]
-        col = coords[1, 0, 0, s]
-        made[n] = jnp.dot(
-            xc[lax.div(col, span), lax.rem(col, per_slab)], upper[s],
-            preferred_element_type=f32,
-        )
-
-    def mirror(n):
-        s = table[5, n]
-        row = lax.rem(coords[0, 0, 0, s], span)
-        made[n] = jnp.dot(
-            xr[lax.div(row, per_slab), lax.rem(row, per_slab)], lower[s],
-            preferred_element_type=f32,
-        )
+    def forward(a, b):
+        def make(n):
+            s = table[4, n]
+            col = coords[1, 0, 0, s]
+            made[n] = jnp.dot(
+                xc[lax.div(col, span), lax.rem(col, per_slab)], upper[s],
+                preferred_element_type=f32,
+            )
+
+        def link(n):
+            cum_f[n + 1] = made[n] + cum_f[table[0, n]]
+
+        running_sums(make, link, a, b)
+
+    def mirror(h, a, b):
+        def row_of(n):
+            return lax.rem(coords[0, 0, 0, table[5, n]], span)
+
+        def make(n):
+            row = row_of(n)
+            out = jnp.dot(
+                xr[h, lax.div(row, per_slab), lax.rem(row, pairs)], lower[table[5, n]],
+                preferred_element_type=f32,
+            )
+            made_m[n, 0] = out[:some]
+            made_m[n, 1] = out[some:]
+
+        def link(n):
+            side = lax.div(lax.rem(row_of(n), per_slab), pairs)
+            cum_m[h, n + 1] = made_m[n, side] + cum_m[h, table[2, n]]
+
+        running_sums(make, link, a, b)
+
+    def pair(h, owner, p):
+        first = owner * per_slab + p
+        return jnp.concatenate(
+            [cum_m[h, table[3, first]], cum_m[h, table[3, first + pairs]]], axis=0
+        )
+
+    def fill_pairs(dst, h, owner, lo, n, *more, to=0):
+        def body(i, _):
+            out = pair(h, owner, lo + i)
+            for source, offset in more:
+                out = out + source[offset + i].astype(f32)
+            dst[to + i] = out.astype(dst.dtype)
+            return 0
+
+        lax.fori_loop(0, n, body, 0, unroll=8)
 
     def fill(dst, cum, at, owner, k, *more, to=None):
         base = k * half
@@ -333,25 +361,121 @@
             fill(z_out.at[2], cum_f, 1, near_end, k, (z_in.at[3], k * half))
             to_end(k).start()
 
-    def to_sib(j):
-        return remote(sib_out.at[j], sib_in.at[j], bs.at[j], br.at[j], sib, c)
-
-    def diag(link):
+    def rows_of(k):
+        return pl.ds(k * quarter, quarter)
+
+    def to_sib(j, h):
         return remote(
-            diag_out.at[link], diag_in.at[link], ds.at[link], dr.at[link], links[link], c
-        )
-
-    def beside_copy(link, i):
+            sib_out.at[h, j], sib_in.at[h, j], bs.at[j, h], br.at[j, h], sib, c
+        )
+
+    def diag(link, h):
+        return remote(
+            diag_out.at[h, link], diag_in.at[h, link], ds.at[link, h], dr.at[link, h],
+            links[link], c,
+        )
+
+    def beside_copy(link, i, h):
         k = link_half(link, i == 0)
         return remote(
-            near_out.at[link, part(k)], near_in.at[link, part(k)],
-            ns.at[link, i], nr.at[link, i], links[link], c,
-        )
-
-    running_sums(forward, cum_f, 0, 0, slots - LATE_COLS)
+            near_out.at[h, link, rows_of(k)], near_in.at[h, link, rows_of(k)],
+            ns.at[link, i, h], nr.at[link, i, h], links[link], c,
+        )
+
+    def give_sib(h):
+        for j, to in enumerate((opposite, beside, across, chip)):
+            fill_pairs(sib_out.at[h, j], h, 2 * to + 1 - core, 0, pairs)
+            to_sib(j, h).start()
+
+    def give_diag(h):
+        to_sib(0, h).wait_recv()
+        for link in range(2):
+            lo = link * quarter
+            fill_pairs(diag_out.at[h, link], h, dn, lo, quarter, (sib_in.at[h, 0], lo))
+            diag(link, h).start()
+
+    def give_first(h):
+        for link in range(2):
+            to_sib(1 + link, h).wait_recv()
+            lo = link_half(link, True) * quarter
+            fill_pairs(
+                near_out.at[h, link], h, links[link], lo, quarter,
+                (sib_in.at[h, 1 + link], lo), to=lo,
+            )
+            beside_copy(link, 0, h).start()
+
+    def give_second(h):
+        for link in range(2):
+            diag(1 - link, h).wait_recv()
+            lo = link_half(link, False) * quarter
+            fill_pairs(
+                near_out.at[h, link], h, links[link], lo, quarter,
+                (sib_in.at[h, 1 + link], lo), (diag_in.at[h, 1 - link], 0), to=lo,
+            )
+            beside_copy(link, 1, h).start()
+
+    def lanes(p):
+        return pl.ds(pl.multiple_of(p * tile, tile), tile)
+
+    def put(h, p, out, keep):
+        rows = pl.ds(h * some, some)
+        for q, value in ((p, out[:some]), (p + pairs, out[some:])):
+            o_ref[rows, lanes(q)] = o_ref[rows, lanes(q)] + value if keep else value
+
+    def base():
+        for h in range(2):
+            to_sib(3, h).wait_recv()
+
+        def body(p, _):
+            at = c * per_slab + p
+            whole = (cum_f[table[1, at]], cum_f[table[1, at + pairs]])
+            for h in range(2):
+                rows = [b[h * some : (h + 1) * some] for b in whole]
+                out = jnp.concatenate(rows, axis=0) + pair(h, r, p)
+                put(h, p, out + sib_in[h, 3, p].astype(f32), False)
+            return 0
+
+        lax.fori_loop(0, pairs, body, 0, unroll=4)
+
+    def add(k, *sources):
+        def body(p, _):
+            at = lanes(k * half + p)
+            out = o_ref[:, at]
+            for source in sources:
+                out = out + source[k * half + p].astype(f32)
+            o_ref[:, at] = out
+            return 0
+
+        lax.fori_loop(0, half, body, 0, unroll=8)
+
+    def take(i, h):
+        for link in range(2):
+            beside_copy(link, i, h).wait_recv()
+            lo = link_half(link, i == 0) * quarter
+
+            def body(p, _):
+                put(h, lo + p, near_in[h, link, lo + p].astype(f32), True)
+                return 0
+
+            lax.fori_loop(0, quarter, body, 0, unroll=8)
+
+    def late_here(h):
+        def body(p, _):
+            xr[h, late_row, p] = xr_late[h, p]
+            return 0
+
+        lax.fori_loop(0, pairs, body, 0, unroll=8)
+
+    early_f, early_m = slots - LATE_COLS, slots - LATE_ROWS
+    forward(0, early_f)
     sib_wait(3, late_col)
-    fetch_late(xc, late_col, xc_late)
-    running_sums(forward, cum_f, 0, slots - LATE_COLS, slots)
+
+    def fetch(p, _):
+        xc[late_col, p] = xc_late[p]
+        return 0
+
+    lax.fori_loop(0, per_slab, fetch, 0, unroll=8)
+    forward(early_f, slots)
 
     @pl.when(end)
     def _():
@@ -359,73 +483,58 @@
             for k in range(2):
                 fill(z_out.at[i], cum_f, 1, owner, k)
                 near(i, k).start()
-
-    @pl.when(end)
-    def _():
         for owner in (next_mid, 3 - next_mid):
-            for k in range(2):
-                z_copy(0, owner, k, next_mid).wait_recv()
-
-    running_sums(mirror, cum_m, 2, 0, slots - LATE_ROWS)
-
-    @pl.when(end)
-    def _():
-        for k in range(2):
-            z_copy(0, late_row, k, next_mid, dst=xr_late).wait_recv()
-
-    fetch_late(xr, late_row, xr_late)
-    running_sums(mirror, cum_m, 2, slots - LATE_ROWS, slots)
-    for j, to in enumerate((opposite, beside, across, chip)):
-        for k in range(2):
-            fill(sib_out.at[j], cum_m, 3, 2 * to + 1 - core, k)
-        to_sib(j).start()
+            for h in range(2):
+                z_copy(0, owner, h, next_mid).wait_recv()
+
+    for h in range(2):
+        mirror(h, 0, early_m)
+
+    def finish_mirror(h):
+        @pl.when(end)
+        def _():
+            z_copy(0, late_row, h, next_mid, dst=xr_late).wait_recv()
+
+        late_here(h)
+        mirror(h, early_m, slots)
+        give_sib(h)
+
+    finish_mirror(0)
+    finish_mirror(1)
     chain_far(0, 0)
-    to_sib(0).wait_recv()
-    for link in range(2):
-        fill(diag_out.at[link], cum_m, 3, dn, link, (sib_in.at[0], link * half), to=0)
-        diag(link).start()
-    for link in range(2):
-        to_sib(1 + link).wait_recv()
-        k = link_half(link, True)
-        fill(near_out.at[link], cum_m, 3, links[link], k, (sib_in.at[1 + link], k * half))
-        beside_copy(link, 0).start()
+    give_diag(0)
+    give_diag(1)
     chain_far(0, 1)
-    for link in range(2):
-        diag(1 - link).wait_recv()
-        k = link_half(link, False)
-        fill(
-            near_out.at[link], cum_m, 3, links[link], k,
-            (sib_in.at[1 + link], k * half), (diag_in.at[1 - link], 0),
-        )
-        beside_copy(link, 1).start()
+    give_first(0)
+    give_first(1)
     chain_end(0)
+    give_second(0)
+    give_second(1)
     chain_far(1, 0)
     chain_end(1)
-    to_sib(3).wait_recv()
-
-    def blocks(body, a, b):
-        def step(p, _):
-            body(p, pl.ds(pl.multiple_of(p * tile, tile), tile))
-            return 0
-
-        lax.fori_loop(a, b, step, 0, unroll=8)
-
-    def base(p, at):
-        o_ref[:, at] = (
-            cum_f[table[1, c * per_slab + p]] + cum_m[table[3, r * per_slab + p]]
-            + sib_in[3, p].astype(f32)
-        )
-
-    def add(k, *sources):
-        def body(p, at):
-            out = o_ref[:, at]
-            for source in sources:
-                out = out + source[p].astype(f32)
-            o_ref[:, at] = out
-
-        blocks(body, k * half, (k + 1) * half)
-
-    blocks(base, 0, per_slab)
+    base()
+    for k in range(2):
+
+        @pl.when(c < 3)
+        def _():
+            z_copy(0, c, k, c + 1).wait_send()
+
+        @pl.when(c > 0)
+        def _():
+            z_copy(1, c, k, c - 1).wait_send()
+
+        @pl.when(mid)
+        def _():
+            z_inner(k).wait_send()
+            z_outer(k).wait_send()
+            z_far(k).wait_send()
+
+        for link in range(2):
+            own_copy(link, r, k).wait_send()
+        for i, owner in enumerate((r, xn, yn, dn)):
+            sib_copy(i, xc.at[owner, part(k)], owner, k).wait_send()
+    for link in range(2):
+        pass_copy(link, links[1 - link]).wait_send()
 
     @pl.when(end)
     def _():
@@ -434,12 +543,9 @@
             add(k, z_in.at[0])
 
     chain_far(1, 1)
-    for link in range(2):
-        beside_copy(link, 0).wait_recv()
-        add(link_half(link, True), near_in.at[link])
-    for link in range(2):
-        beside_copy(link, 1).wait_recv()
-        add(link_half(link, False), near_in.at[link])
+    for h in range(2):
+        for i in range(2):
+            take(i, h)
 
     @pl.when(mid)
     def _():
@@ -448,41 +554,23 @@
             near(2, k).wait_recv()
             add(k, z_in.at[4], z_in.at[2])
 
-    for k in range(2):
-
-        @pl.when(c < 3)
-        def _():
-            z_copy(0, c, k, c + 1).wait_send()
-
-        @pl.when(c > 0)
-        def _():
-            z_copy(1, c, k, c - 1).wait_send()
-
-        @pl.when(mid)
-        def _():
-            z_inner(k).wait_send()
-            z_outer(k).wait_send()
-            z_far(k).wait_send()
-
-        for i in range(3):
+    for i in range(3):
+        for k in range(2):
             near(i, k).wait_send()
+    for h in range(2):
         for link in range(2):
-            own_copy(link, r, k).wait_send()
-            beside_copy(link, k).wait_send()
-        for i, owner in enumerate((r, xn, yn, dn)):
-            sib_copy(i, xc.at[owner, part(k)], owner, k).wait_send()
-    for link in range(2):
-        pass_copy(link, links[1 - link]).wait_send()
-        diag(link).wait_send()
-    for j in range(4):
-        to_sib(j).wait_send()
+            diag(link, h).wait_send()
+            for i in range(2):
+                beside_copy(link, i, h).wait_send()
+        for j in range(4):
+            to_sib(j, h).wait_send()
 
 
 def fused(tiles, tile_coords, tile_counts, x):
     slots, tile = tiles.shape[2], tiles.shape[-1]
     vecs, width = x.shape
     slab = width // tile
-    half = slab // 2
+    pairs, some = slab // 2, vecs // 2
     dma, bf16, f32, i32 = pltpu.SemaphoreType.DMA, jnp.bfloat16, jnp.float32, jnp.int32
 
     def blocks(*lead, dtype=bf16):
@@ -495,25 +583,26 @@
         out_specs=pl.BlockSpec(memory_space=pltpu.VMEM),
         scratch_shapes=[
             pltpu.VMEM(x.shape, bf16),
-            blocks(4, slab),
+            blocks(2, 4, pairs),
             blocks(8, slab),
-            blocks(slab),
+            blocks(2, pairs),
             blocks(slab),
             pltpu.VMEM((slots, tile, tile), bf16),
             pltpu.VMEM((slots, tile, tile), bf16),
             pltpu.VMEM((2, tile, tile), bf16),
             blocks(slots, dtype=f32),
+            pltpu.VMEM((slots, 2, some, tile), f32),
             blocks(slots + 1, dtype=f32),
-            blocks(slots + 1, dtype=f32),
+            pltpu.VMEM((2, slots + 1, some, tile), f32),
             pltpu.VMEM((8, 8 * slab), i32),
             blocks(3, slab),
             blocks(5, slab),
-            blocks(4, slab),
-            blocks(4, slab),
-            blocks(2, half),
-            blocks(2, half),
-            blocks(2, slab),
-            blocks(2, slab),
+            blocks(2, 4, pairs),
+            blocks(2, 4, pairs),
+            blocks(2, 2, pairs // 2),
+            blocks(2, 2, pairs // 2),
+            blocks(2, 2, pairs),
+            blocks(2, 2, pairs),
             pltpu.SMEM(tile_coords.shape, i32),
             pltpu.VMEM(tile_coords.shape, i32),
             pltpu.VMEM((1, 1), i32),
@@ -524,9 +613,9 @@
             dma((2, 3)), dma((2, 3)),
             dma((4, 2)), dma((4, 2)),
             dma((3, 2)), dma((5, 2)),
-            dma((4,)), dma((4,)),
-            dma((2,)), dma((2,)),
+            dma((4, 2)), dma((4, 2)),
             dma((2, 2)), dma((2, 2)),
+            dma((2, 2, 2)), dma((2, 2, 2)),
         ],
         compiler_params=pltpu.CompilerParams(
             collective_id=0, has_side_effects=True, vmem_limit_bytes=VMEM_LIMIT

time: 37.7 us -> 36.7 us (0.973)
  Pallas kernels: 36.2 us -> 35.1 us
    pallas_call x1, Pallas kernels: 36.2 us -> 35.1 us  [fused(): pl.pallas_call(fused_kernel, out_shape=jax.ShapeDtypeStruct(x.shape, f32)...]
where the time goes in v4:
time: 36.7 us; the launch traced here: 36.5 us
  Pallas kernels  35.1 us (96%)
  local copies, waits for them, and re-layouts  0.8 us (2%)
  between operations  0.66 us (2%)
    pallas_call x1, Pallas kernels, fused(): pl.pallas_call(fused_kernel, out_shape=jax.ShapeDtypeStruct(x.shape, f32)...  35.1 us
    unnamed x1, local copies, waits for them, and re-layouts  0.8 us

profile of v4, /device:TPU:0, one launch (start us, length us, event | category | flops | bytes accessed | tf_op | source)
XLA Modules:
  0.0 36.5 jit_solution(5337259496803814512)
XLA Ops:
  0.7 35.1 %fused_product.1 = f32[16,8192]{1,0:T(8,128)S(1)} custom-call(s32[2,1,1,80]{3,2,1,0:T(1,128)} %coords_hbm.1, s32[1,1]{1,0:T(1,128)S(6)} %copy.6.count_hbm, bf16[16,8192]{1,0:T(8,128)(2,1)} %bitcast.3, bf16[1,1,80,256,256]{4,3,2,1,0:T(8,128)(2,1)} %t_ref.1), custom_call_target="tpu_custom_call" | custom-call | tf_op jit(solution)/shard_map/fused_product/pallas_call | solution.py:579
  35.8 0.8 %copy.7 = f32[8192,16]{0,1:T(8,128)} copy(f32[8192,16]{0,1:T(8,128)S(1)} %bitcast.2) | data formatting | bytes 1048576
